TPU v7x, 32 devices: a whole 2x2x4 slice. The times are simulated.
32 devices in a mesh: stn: 8 (over z, y), grid: 4 (over x, core).
Axes of the slice: x: 2, y: 2, z: 4, core: 2. Of those that a mesh axis runs over, the one named last changes fastest.
Arguments:
- voltages: bfloat16 [512, 2, 12288], P('stn', None, 'grid'), may hold values from -6 to 6
- pfb_coeffs: float32 [16, 48], replicated, may hold values from -1.5 to 1.5
- station_offsets: int32 [2, 512], replicated, may hold values from 0 to 4
- tile_cells: int32 [24, 2, 136], P('stn'), may hold values from 0 to 127, as said below
- kernel_table: float32 [8, 7], replicated, may hold values from 0.2 to 1
Outputs:
- uv_grid: float32 [128, 24, 256], P('grid', 'stn')
Inputs may be any that keep to these rules, and one draw needn't show every extreme that they name: tile_cells[c, 0, k] lies in one of the strips of 32 rows; in every channel at most 68 baseline tiles have their base row in the same strip, and one strip holds exactly 68. A base row in the last strip and every base column are at most 112.
All inputs are finite; a program needn't handle non-finite values.
Results may differ from a plain program's by a relative error of at most 0.0065.
Values may be sent and summed in bfloat16 or wider, within the bound.
A program may use at most 128 MiB of HBM per device.

v0:
```python
import math
import jax
import jax.numpy as jnp
import numpy as np
from jax import lax
from jax.sharding import PartitionSpec as P

TILE = 32
PATCH = 16
SPREAD = 5
UV = 128
highest = lax.Precision.HIGHEST


def shifted(block, axis, distance):
    devices = range(lax.axis_size(axis))
    route = [(i - distance, i) for i in devices if i - distance in devices]
    return lax.ppermute(block, axis, route)


def dft_table(frame_len):
    chan_count = frame_len // 2
    sample_line = jnp.arange(frame_len, dtype=jnp.int32)[:, None]
    chan_line = jnp.arange(chan_count, dtype=jnp.int32)[None, :]
    angles = (sample_line * chan_line % frame_len).astype(jnp.float32) * (2.0 * math.pi / frame_len)
    norm_factor = 1.0 / math.sqrt(frame_len)
    twiddle = jnp.stack([jnp.cos(angles) * norm_factor, -jnp.sin(angles) * norm_factor], axis=2)
    return twiddle.reshape(frame_len, 2 * chan_count).astype(jnp.bfloat16)


CLASSES = 32
high = lax.Precision.HIGH


def fused_filter(coeffs, twiddle, step):
    taps, frame_len = coeffs.shape
    flat = coeffs.reshape(-1)
    columns = [
        jnp.pad(flat, (frame_len * (f + 1), frame_len * (step - 1 - f))) for f in range(step)
    ]
    shifted_coeffs = jnp.stack(columns, axis=0)
    spread = np.kron(np.ones((1, frame_len), np.float32), np.eye(step, dtype=np.float32))
    wide = jnp.einsum("fm,fn->mn", shifted_coeffs, jnp.asarray(spread), precision=highest)
    tiled = jnp.tile(jnp.repeat(twiddle.astype(jnp.float32), step, axis=1), (step + taps, 1))
    return (wide * tiled).astype(jnp.bfloat16)


def separation_table(frequency, divisor, kernel_table):
    over_count = kernel_table.shape[0]
    separation = jnp.arange(2 * SPREAD - 1, dtype=jnp.int32)
    scaled = separation * frequency
    cell_index = scaled // divisor
    fine_index = scaled % divisor * over_count // divisor
    choose = (fine_index[:, None] == jnp.arange(over_count, dtype=jnp.int32)[None, :]).astype(
        jnp.float32
    )
    tap_values = jnp.dot(choose, kernel_table, precision=highest)
    place_rel = jnp.arange(PATCH, dtype=jnp.int32)[None, :] - cell_index[:, None]
    weights = jnp.zeros(place_rel.shape, jnp.float32)
    for tap_index in range(kernel_table.shape[1]):
        weights = weights + tap_values[:, tap_index : tap_index + 1] * (
            place_rel == tap_index
        ).astype(jnp.float32)
    return weights


def joint_weights(frequencies, divisor, kernel_table):
    class_line = np.arange(CLASSES)
    class_u = np.minimum(class_line // SPREAD, SPREAD - 1)
    class_v = class_line % SPREAD
    sep_line = np.arange(2 * SPREAD - 1)
    pick_u = (class_u[:, None] - class_u[None, :] + SPREAD - 1).reshape(-1, 1) == sep_line
    pick_v = (class_v[:, None] - class_v[None, :] + SPREAD - 1).reshape(-1, 1) == sep_line
    weights = jnp.stack([separation_table(f, divisor, kernel_table) for f in frequencies])
    over_r = np.kron(np.eye(PATCH), np.ones((1, PATCH))).astype(np.float32)
    over_t = np.kron(np.ones((1, PATCH)), np.eye(PATCH)).astype(np.float32)
    wide_u = jnp.einsum("czr,rm->czm", weights, jnp.asarray(over_r), precision=highest)
    wide_v = jnp.einsum("czr,rm->czm", weights, jnp.asarray(over_t), precision=highest)
    full_u = jnp.einsum(
        "qz,czm->cqm", jnp.asarray(pick_u.astype(np.float32)), wide_u, precision=highest
    )
    full_v = jnp.einsum(
        "qz,czm->cqm", jnp.asarray(pick_v.astype(np.float32)), wide_v, precision=highest
    )
    return full_u * full_v


def body(voltages, pfb_coeffs, station_offsets, tile_cells, kernel_table):
    stn_local, pol_count, samples = voltages.shape
    tap_count, frame_len = pfb_coeffs.shape
    spec_count = samples // frame_len
    step = 128 // math.gcd(128, frame_len)
    chunks = spec_count // step
    flat = voltages.reshape(stn_local * pol_count, samples)
    earlier = shifted(flat[:, samples - tap_count * frame_len :], "grid", 1)
    extended = jnp.concatenate([earlier, flat], axis=1)
    width = step * frame_len
    reach = (step + tap_count) * frame_len
    blocks = jnp.stack([extended[:, c * width : c * width + reach] for c in range(chunks)], axis=1)
    matrix = fused_filter(pfb_coeffs, dft_table(frame_len), step)
    spectra = jnp.einsum("rcm,mn->nrc", blocks, matrix, preferred_element_type=jnp.float32).astype(
        jnp.bfloat16
    )
    spectra = spectra.reshape(frame_len // 2, 2, step, stn_local, pol_count * chunks)
    spectra = jnp.transpose(spectra, (0, 1, 3, 2, 4)).reshape(
        frame_len // 2, 2, stn_local, step * pol_count * chunks
    )
    turned = lax.all_to_all(spectra, "stn", split_axis=0, concat_axis=2, tiled=True)
    ch_dev, _, stations, depth = turned.shape
    tiles = stations // TILE
    divisor = frame_len - 1
    first_chan = lax.axis_index("stn") * ch_dev + frame_len // 2
    norm_factor = 1.0 / (pol_count * spec_count * lax.axis_size("grid"))
    classes = (station_offsets[0] * SPREAD + station_offsets[1]).reshape(tiles, TILE)
    hot = classes[:, :, None] == jnp.arange(CLASSES, dtype=jnp.int32)
    hot_low = hot.astype(jnp.bfloat16)
    hot_full = hot.astype(jnp.float32)
    tiled = turned.reshape(ch_dev, 2, tiles, TILE, depth)
    summed = jnp.einsum(
        "aiq,ceaik->ceaqk", hot_low, tiled, preferred_element_type=jnp.float32
    ).astype(jnp.bfloat16)

    def stacked(z):
        real_part, imag_part = (z[:, 0], z[:, 1])
        partner = jnp.concatenate([real_part, imag_part], axis=-1)
        turned_partner = jnp.concatenate([imag_part, -real_part], axis=-1)
        return (jnp.stack([partner, turned_partner], axis=1), partner)

    left, right = stacked(summed)
    cross = jnp.einsum("ceaqk,cbsk->ceabqs", left, right, preferred_element_type=jnp.float32)
    joint = joint_weights([first_chan + i for i in range(ch_dev)], divisor, kernel_table)
    joint = joint * norm_factor
    patch = jnp.einsum(
        "ceabm,cmn->ceabn",
        cross.reshape(ch_dev, 2, tiles, tiles, CLASSES * CLASSES),
        joint,
        precision=high,
    )
    own_left, own_right = stacked(tiled)
    own = jnp.einsum("ceaik,cajk->ceaij", own_left, own_right, preferred_element_type=jnp.float32)
    line = np.arange(TILE)
    own = jnp.where(jnp.asarray(line[:, None] < line[None, :]), own, 0.0)
    own = jnp.einsum("aiq,ceaij->ceaqj", hot_full, own, precision=high)
    own = jnp.einsum("ceaqj,ajs->ceaqs", own, hot_full, precision=high)
    own_patch = jnp.einsum(
        "ceam,cmn->cean", own.reshape(ch_dev, 2, tiles, CLASSES * CLASSES), joint, precision=high
    )
    same = np.eye(tiles, dtype=bool)[:, :, None]
    patch = jnp.where(jnp.asarray(same), own_patch[:, :, :, None, :], patch)
    pair_first, pair_second = np.triu_indices(tiles)
    select = np.zeros((pair_first.size, tiles * tiles), np.float32)
    select[np.arange(pair_first.size), pair_first * tiles + pair_second] = 1.0
    missing = (1.0 - select.sum(axis=0)).astype(np.int32) * 4096
    cells = jnp.einsum(
        "cxk,kp->cxp", tile_cells.astype(jnp.float32), jnp.asarray(select), precision=highest
    )
    cells = jnp.round(cells).astype(jnp.int32) + jnp.asarray(missing)
    patch = patch.reshape(ch_dev, 2, tiles * tiles, PATCH, PATCH)
    patch_line = jnp.arange(PATCH, dtype=jnp.int32)
    target = cells[..., None] + patch_line
    spots = (target[..., None] == jnp.arange(UV, dtype=jnp.int32)).astype(jnp.float32)
    rows, cols = (spots[:, 0], spots[:, 1])
    spread_cols = jnp.einsum("cekrt,cktw->ckrew", patch, cols, precision=high)
    planes = jnp.einsum("ckru,ckrew->ucew", rows, spread_cols, precision=high)
    planes = planes.reshape(UV, ch_dev, 2 * UV)
    return lax.psum_scatter(planes, "grid", scatter_dimension=0, tiled=True)


def solution(mesh):
    placed = (P("stn", None, "grid"), P(), P(), P("stn", None, None), P())
    return jax.shard_map(
        body, mesh=mesh, in_specs=placed, out_specs=P("grid", "stn", None), check_vma=False
    )
```

profile of v0, /device:TPU:0, one launch (start us, length us, event | category | flops | bytes accessed | tf_op | source)
XLA Modules:
  0.0 228.6 jit_solution(5774973549644276165)
XLA Ops:
  6.5 2.3 %reshape.1055 = bf16[128,3072]{1,0:T(8,128)(2,1)S(1)} reshape(bf16[64,2,3072]{2,1,0:T(2,128)(2,1)} %param.14) | data formatting | bytes 1572864 | tf_op jit(solution)/shard_map/reshape | solution.py:94
  8.9 2.4 %collective-permute-start = (bf16[128,768]{1,0:T(8,128)(2,1)S(1)}, bf16[128,768]{1,0:T(8,128)(2,1)S(1)}, u32[]{:S(2)}, u32[]{:S(2)}) collective-permute-start(bf16[128,768]{1,0:T(8,128)(2,1)S(1)} %slice.161), channel_id=1, source_target_pairs={{0,1},{1,2},{2,3},{4,5},{5,6},{6,7},{8,9},{9,10},{10,11},{12,13},{... | collective-permute-start | bytes 589832 | tf_op jit(solution)/shard_map/ppermute | solution.py:18
  11.4 0.1 reshape.1054
  11.5 0.1 fusion.98
  11.6 0.1 copy.101
  11.8 0.2 fusion.82
  12.0 0.2 fusion.81
  12.3 0.2 fusion.80
  12.5 0.1 select_add_fusion
  12.6 0.1 select_add_fusion.1
  12.8 0.1 select_add_fusion.2
  12.9 0.2 fusion.53
  13.1 4.3 %fusion.99 = f32[3,256,1024]{2,1,0:T(8,128)} fusion(f32[3,9,256]{2,1,0:T(8,128)S(1)} %fusion.53, f32[1024,9,1]{0,1,2:T(8,128)S(1)} %copy-done.7), kind=kOutput, calls=%fused_computation.178 | convolution fusion | flops 84934656 | bytes 3210240 | tf_op jit(solution)/shard_map/qz,czm->cqm/dot_general | solution.py:79
  17.4 0.2 fusion.29
  17.7 1.3 fusion.8
  19.0 0.2 fusion.52
  19.5 1.2 convolution_convert_fusion.1
  20.8 0.5 copy.103
  21.3 15.6 %reshape.1056 = bf16[24,2,8,64,16]{2,1,0,4,3:T(2,128)(2,1)} reshape(bf16[384,128,8]{0,2,1:T(8,128)(2,1)S(1)} %copy.103) | data formatting | bytes 1572864 | tf_op jit(solution)/shard_map/reshape | solution.py:104
  37.0 30.5 %copy.104 = bf16[24,2,64,8,16]{2,4,3,1,0:T(8,128)(2,1)S(1)} copy(bf16[24,2,64,8,16]{3,1,0,4,2:T(2,128)(2,1)} %bitcast.218) | data formatting | bytes 1572864 | tf_op jit(solution)/shard_map/transpose | solution.py:105
  67.5 1.4 copy.105
  68.9 6.8 %all-to-all-start = ((bf16[24,2,64,128]{3,2,1,0:T(8,128)(2,1)}), bf16[24,2,64,128]{3,2,1,0:T(8,128)(2,1)}, u32[]{:S(2)}, u32[]{:S(2)}) async-start(bf16[24,2,64,128]{3,2,1,0:T(8,128)(2,1)} %copy.105), calls=%async_computation | async-start | bytes 1572864 | tf_op jit(solution)/shard_map/all_to_all | solution.py:108
  75.7 0.2 reduce-scatter.2.cloned.1.call-start
  76.0 0.1 add.327
  76.1 0.3 iota_add_fusion
  76.3 4.7 %multiply_multiply_fusion = f32[3,256,1024]{2,1,0:T(8,128)S(1)} fusion(f32[3,256,1024]{2,1,0:T(8,128)} %fusion.99, f32[3,9,256]{2,1,0:T(8,128)S(1)} %fusion.52, f32[1024,9,1]{0,1,2:T(8,128)S(1)} %copy-done.6), kind=kOutput, calls=%fused_computation.12 | convolution fusion | flops 86507520 | bytes 6355968 | tf_op jit(solution)/shard_map/qz,czm->cqm/dot_general | solution.py:82
  81.1 5.4 %iota_compare_fusion = pred[3,2,256,16,128]{4,3,2,0,1:T(8,128)(4,1)} fusion(s32[3,2,256,16]{3,2,0,1:T(8,128)S(1)} %iota_add_fusion), kind=kLoop, calls=%fused_computation.4 | loop fusion | flops 3145728 | bytes 3244032 | tf_op jit(solution)/shard_map/eq | solution.py:161
  86.5 10.8 %all-to-all-done = bf16[24,2,64,128]{3,2,1,0:T(8,128)(2,1)} async-done(((bf16[24,2,64,128]{3,2,1,0:T(8,128)(2,1)}), bf16[24,2,64,128]{3,2,1,0:T(8,128)(2,1)}, u32[]{:S(2)}, u32[]{:S(2)}) %all-to-all-start) | async-done | bytes 786464 | tf_op jit(solution)/shard_map/all_to_all | solution.py:108
  97.3 1.2 copy.106
  98.5 0.4 fusion.26
  99.0 1.0 slice_bitcast_fusion.7
  100.0 0.3 fusion.34
  100.3 10.1 %convolution_bitcast_fusion = f32[3,2,16,16,32,32]{4,5,2,1,3,0:T(8,128)} fusion(bf16[3,16,32,256,1,1]{3,2,0,1,5,4:T(8,128)(2,1)S(1)} %get-tuple-element.7, bf16[3,1,16,32,256]{4,3,0,2,1:T(8,128)(2,1)S(1)} %get-tuple-element.13, bf16[3,1,16,32,256]{4,3,0,2,1:T(8,128)(2,1)S(1)} %get-tuple-element.8), kind=kOutput, calls=%fused_computation.5 | convolution fusion | flops 806092800 | bytes 8650752 | tf_op jit(solution)/shard_map/ceaqk,cbsk->ceabqs/dot_general | solution.py:130
  110.4 24.9 %copy.118 = f32[3,2,16,16,32,32]{5,4,3,2,1,0:T(8,128)} copy(f32[3,2,16,16,32,32]{4,5,2,1,3,0:T(8,128)} %convolution_bitcast_fusion) | data formatting | bytes 12582912 | tf_op jit(solution)/shard_map/ceaqk,cbsk->ceabqs/transpose | solution.py:130
  135.3 19.9 %reshape.1060 = f32[3,2,16,16,1024]{4,3,2,1,0:T(8,128)} reshape(f32[3,2,16,16,32,32]{5,4,3,2,1,0:T(8,128)} %copy.118) | data formatting | bytes 12582912 | tf_op jit(solution)/shard_map/reshape | solution.py:135
  155.3 1.6 fusion.36
  156.9 1.3 bitcast_select_fusion
  158.2 0.6 fusion.16
  158.8 1.7 fusion.18
  160.6 3.0 %copy.113 = f32[3,2,16,32,32]{4,3,2,1,0:T(8,128)} copy(f32[3,2,16,32,32]{3,4,1,0,2:T(8,128)} %fusion.18) | data formatting | bytes 786432 | tf_op jit(solution)/shard_map/ceaqj,ajs->ceaqs/transpose | solution.py:144
  163.6 2.1 reshape.1059
  165.7 1.5 fusion.6
  167.3 6.8 %fusion.23 = f32[3,2,16,16,256]{4,3,2,1,0:T(8,128)} fusion(f32[3,2,16,16,1024]{4,3,2,1,0:T(8,128)} %reshape.1060, f32[3,256,1024]{2,1,0:T(8,128)S(1)} %multiply_multiply_fusion, f32[3,2,16,256]{3,2,1,0:T(8,128)S(1)} %fusion.6, pred[16,16]{1,0:T(8,128)(4,1)S(1)} %copy-done.11), kind=kOutput, calls=%fused_computation.34 | convolution fusion | flops 2416312320 | bytes 11108608 | tf_op jit(solution)/shard_map/ceabm,cmn->ceabn/dot_general | solution.py:133
  174.1 8.4 %reshape.1061 = f32[3,2,256,16,16]{4,3,2,1,0:T(8,128)} reshape(f32[3,2,16,16,256]{4,3,2,1,0:T(8,128)} %fusion.23) | data formatting | bytes 3145728 | tf_op jit(solution)/shard_map/reshape | solution.py:158
  182.5 9.3 %fusion.2 = f32[3,256,128,2,16]{2,4,3,1,0:T(8,128)} fusion(f32[3,2,256,16,16]{4,3,2,1,0:T(8,128)} %reshape.1061, pred[3,2,256,16,128]{4,3,2,0,1:T(8,128)(4,1)S(1)} %copy-done.2), kind=kOutput, calls=%fused_computation.2 | convolution fusion | flops 301989888 | bytes 15728640 | tf_op jit(solution)/shard_map/cekrt,cktw->ckrew/dot_general | solution.py:163
  191.8 9.8 %fusion = f32[3,2,128,128,1]{3,2,1,4,0:T(8,128)S(1)} fusion(f32[3,256,128,2,16]{2,4,3,1,0:T(8,128)} %fusion.2, pred[3,2,256,16,128]{4,3,2,0,1:T(8,128)(4,1)S(1)} %copy-done.2), kind=kOutput, calls=%fused_computation | convolution fusion | flops 2415919104 | bytes 14548992 | tf_op jit(solution)/shard_map/ckru,ckrew->ucew/dot_general | solution.py:164
  201.7 0.9 copy.121
  202.6 19.1 %reduce-scatter.2.cloned.1.call-done = f32[32,3,256]{2,0,1:T(8,128)} async-done(((f32[128,3,256]{2,0,1:T(8,128)}), f32[32,3,256]{2,0,1:T(8,128)}) %reduce-scatter.2.cloned.1.call-update) | async-done | bytes 98320 | tf_op jit(solution)/shard_map/reduce_scatter | solution.py:166
  (76 shorter events, 0.9 us)
Async XLA Ops:
  6.5 5.2 %copy-start = (f32[8,7]{1,0:T(8,128)S(1)}, f32[8,7]{1,0:T(8,128)}, u32[]{:S(2)}) copy-start(f32[8,7]{1,0:T(8,128)} %param.18) | copy-start | bytes 676
  6.5 6.3 %copy-start.9 = (f32[16,256,1]{1,0,2:T(8,128)S(1)}, f32[16,256,1]{1,0,2:T(8,128)}, u32[]{:S(2)}) copy-start(f32[16,256,1]{1,0,2:T(8,128)} %constant.175) | copy-start | bytes 49156
  6.5 6.5 %copy-start.7 = (f32[1024,9,1]{0,1,2:T(8,128)S(1)}, f32[1024,9,1]{0,1,2:T(8,128)}, u32[]{:S(2)}) copy-start(f32[1024,9,1]{0,1,2:T(8,128)} %constant.176) | copy-start | bytes 110596
  6.5 4.8 %copy-start.10 = (f32[16,48]{1,0:T(8,128)S(1)}, f32[16,48]{1,0:T(8,128)}, u32[]{:S(2)}) copy-start(f32[16,48]{1,0:T(8,128)} %param.15) | copy-start | bytes 9220
  6.5 5.9 %copy-start.12 = (s32[3,2,136]{2,1,0:T(2,128)S(1)}, s32[3,2,136]{2,1,0:T(2,128)}, u32[]{:S(2)}) copy-start(s32[3,2,136]{2,1,0:T(2,128)} %param.17) | copy-start | bytes 9796
  8.9 10.2 %collective-permute-start = (bf16[128,768]{1,0:T(8,128)(2,1)S(1)}, bf16[128,768]{1,0:T(8,128)(2,1)S(1)}, u32[]{:S(2)}, u32[]{:S(2)}) collective-permute-start(bf16[128,768]{1,0:T(8,128)(2,1)S(1)} %slice.161), channel_id=1, source_target_pairs={{0,1},{1,2},{2,3},{4,5},{5,6},{6,7},{8,9},{9,10},{10,11},{12,13},{... | collective-permute-start | bytes 589832 | tf_op jit(solution)/shard_map/ppermute | solution.py:18
  12.2 5.2 %copy-start.5 = (f32[136,256,1]{1,0,2:T(8,128)S(1)}, f32[136,256,1]{1,0,2:T(8,128)}, u32[]{:S(2)}) copy-start(f32[136,256,1]{1,0,2:T(8,128)} %constant.174) | copy-start | bytes 417796
  12.2 5.2 %copy-start.22 = (s32[256]{0:T(256)S(1)}, s32[256]{0:T(256)}, u32[]{:S(2)}) copy-start(s32[256]{0:T(256)} %constant.139.clone) | copy-start | bytes 3076
  12.7 4.9 %copy-start.14 = (f32[384]{0:T(512)S(1)}, f32[384]{0:T(512)}, u32[]{:S(2)}) copy-start(f32[384]{0:T(512)} %constant.173) | copy-start | bytes 4612
  12.7 4.9 %copy-start.15 = (f32[384]{0:T(512)S(1)}, f32[384]{0:T(512)}, u32[]{:S(2)}) copy-start(f32[384]{0:T(512)} %constant.171) | copy-start | bytes 4612
  12.7 4.9 %copy-start.16 = (f32[384]{0:T(512)S(1)}, f32[384]{0:T(512)}, u32[]{:S(2)}) copy-start(f32[384]{0:T(512)} %constant.169) | copy-start | bytes 4612
  12.7 4.9 %copy-start.17 = (f32[384]{0:T(512)S(1)}, f32[384]{0:T(512)}, u32[]{:S(2)}) copy-start(f32[384]{0:T(512)} %constant.167) | copy-start | bytes 4612
  12.7 4.9 %copy-start.18 = (f32[384]{0:T(512)S(1)}, f32[384]{0:T(512)}, u32[]{:S(2)}) copy-start(f32[384]{0:T(512)} %constant.165) | copy-start | bytes 4612
  12.7 4.9 %copy-start.19 = (f32[384]{0:T(512)S(1)}, f32[384]{0:T(512)}, u32[]{:S(2)}) copy-start(f32[384]{0:T(512)} %constant.163) | copy-start | bytes 4612
  12.7 4.9 %copy-start.20 = (f32[384]{0:T(512)S(1)}, f32[384]{0:T(512)}, u32[]{:S(2)}) copy-start(f32[384]{0:T(512)} %constant.161) | copy-start | bytes 4612
  12.8 4.9 %copy-start.21 = (f32[384]{0:T(512)S(1)}, f32[384]{0:T(512)}, u32[]{:S(2)}) copy-start(f32[384]{0:T(512)} %constant.159) | copy-start | bytes 4612
  13.1 5.9 %copy-start.8 = (f32[16,256,1]{1,0,2:T(8,128)S(1)}, f32[16,256,1]{1,0,2:T(8,128)}, u32[]{:S(2)}) copy-start(f32[16,256,1]{1,0,2:T(8,128)} %constant.177) | copy-start | bytes 49156
  67.5 8.4 %copy-start.13 = (s32[2,512]{1,0:T(2,128)S(1)}, s32[2,512]{1,0:T(2,128)}, u32[]{:S(2)}) copy-start(s32[2,512]{1,0:T(2,128)} %param.16) | copy-start | bytes 12292
  68.9 7.4 %copy-start.6 = (f32[1024,9,1]{0,1,2:T(8,128)S(1)}, f32[1024,9,1]{0,1,2:T(8,128)}, u32[]{:S(2)}) copy-start(f32[1024,9,1]{0,1,2:T(8,128)} %constant.178) | copy-start | bytes 110596
  68.9 28.4 %all-to-all-start = ((bf16[24,2,64,128]{3,2,1,0:T(8,128)(2,1)}), bf16[24,2,64,128]{3,2,1,0:T(8,128)(2,1)}, u32[]{:S(2)}, u32[]{:S(2)}) async-start(bf16[24,2,64,128]{3,2,1,0:T(8,128)(2,1)} %copy.105), calls=%async_computation | async-start | bytes 1572864 | tf_op jit(solution)/shard_map/all_to_all | solution.py:108
  75.7 146.0 %reduce-scatter.2.cloned.1.call-start = ((), (), s32[]{:S(2)}) async-start(), calls=%async_computation.2 | async-start | bytes 491520 | tf_op jit(solution)/shard_map/reduce_scatter | solution.py:166
  155.3 1.6 copy-start.3
  155.3 1.6 copy-start.4
  155.3 1.7 copy-start.23
  165.7 1.6 copy-start.11
  174.1 8.4 %copy-start.2 = (pred[3,2,256,16,128]{4,3,2,0,1:T(8,128)(4,1)S(1)}, pred[3,2,256,16,128]{4,3,2,0,1:T(8,128)(4,1)}, u32[]{:S(2)}) copy-start(pred[3,2,256,16,128]{4,3,2,0,1:T(8,128)(4,1)} %iota_compare_fusion) | copy-start | bytes 9437188
  191.8 29.9 %copy-start.1 = (f32[8,7]{1,0:T(8,128)S(1)}, f32[8,7]{1,0:T(8,128)}, u32[]{:S(2)}) copy-start(f32[8,7]{1,0:T(8,128)} %param.18) | copy-start | bytes 676
Sparse Core Ops, SparseCore 0:
  202.7 18.9 reduce-scatter.1
where the time goes:
time: 230 us; the launch traced here: 229 us
  local copies, waits for them, and re-layouts  113 us (49%)
  matrix products  53 us (23%)
  waiting for transfers between devices  30 us (13%)
  between operations  14 us (6%)
  other arithmetic  9.47 us (4%)
  starting transfers between devices  9.38 us (4%)
    transpose x1, local copies, waits for them, and re-layouts, body(): jnp.transpose(spectra, (0, 1, 3, 2, 4))  30.5 us
    transpose x1, local copies, waits for them, and re-layouts, body(): jnp.einsum('ceaqk,cbsk->ceabqs', left, right, preferred_element_type=jnp....  24.9 us
    reshape x1, local copies, waits for them, and re-layouts, body(): cross.reshape(ch_dev, 2, tiles, tiles, CLASSES * CLASSES)  19.9 us
    reduce_scatter x1, waiting for transfers between devices, body(): return lax.psum_scatter(planes, 'grid', scatter_dimension=0, tiled=True)  19.1 us
    reshape x1, local copies, waits for them, and re-layouts, body(): spectra.reshape(frame_len // 2, 2, step, stn_local, pol_count * chunks)  15.6 us
    all_to_all x1, waiting for transfers between devices, body(): lax.all_to_all(spectra, 'stn', split_axis=0, concat_axis=2, tiled=True)  10.8 us
    dot_general x1, matrix products, body(): jnp.einsum('ceaqk,cbsk->ceabqs', left, right, preferred_element_type=jnp....  10.1 us
    dot_general x1, matrix products, body(): planes = jnp.einsum('ckru,ckrew->ucew', rows, spread_cols, precision=high)  9.85 us
  transfers between devices with their start and end apart: 3, of which 2 were waited for; matrix products, arithmetic and copies ran while one was open for 8% of the time, Pallas kernels for 0%

commit v1 on v0

--- a/solution.py
+++ b/solution.py
@@ -1,3 +1,4 @@
+import functools
 import math
 import jax
 import jax.numpy as jnp
@@ -10,6 +11,21 @@
 SPREAD = 5
 UV = 128
 highest = lax.Precision.HIGHEST
+
+
+def yards_fix(array_here, axis_tag):
+    return jnp.concatenate(
+        lax.all_to_all(
+            jnp.stack(jnp.split(array_here, lax.axis_size(axis_tag), 0)),
+            axis_name=axis_tag,
+            split_axis=0,
+            concat_axis=0,
+        ),
+        2,
+    )
+
+
+finish_the_bands = functools.partial(yards_fix, axis_tag="stn")
 
 
 def shifted(block, axis, distance):
@@ -105,7 +121,7 @@
     spectra = jnp.transpose(spectra, (0, 1, 3, 2, 4)).reshape(
         frame_len // 2, 2, stn_local, step * pol_count * chunks
     )
-    turned = lax.all_to_all(spectra, "stn", split_axis=0, concat_axis=2, tiled=True)
+    turned = finish_the_bands(spectra)
     ch_dev, _, stations, depth = turned.shape
     tiles = stations // TILE
     divisor = frame_len - 1

time: 230 us -> 254 us (1.10)
  local copies, waits for them, and re-layouts: 113 us -> 135 us
    split x0 -> x9, local copies, waits for them, and re-layouts: none -> 47 us  [yards_fix(): jnp.split(array_here, lax.axis_size(axis_tag), 0)]
    transpose x1 -> x0, local copies, waits for them, and re-layouts: 30.5 us -> none  [body(): jnp.transpose(spectra, (0, 1, 3, 2, 4))]
    unnamed x56 -> x69, local copies, waits for them, and re-layouts: 0.37 us -> 5.88 us
where the time goes in v1:
time: 254 us; the launch traced here: 252 us
  local copies, waits for them, and re-layouts  135 us (53%)
  matrix products  54.2 us (21%)
  waiting for transfers between devices  29.9 us (12%)
  between operations  14 us (6%)
  other arithmetic  9.45 us (4%)
  starting transfers between devices  9.38 us (4%)
    split x9, local copies, waits for them, and re-layouts, yards_fix(): jnp.split(array_here, lax.axis_size(axis_tag), 0)  47 us
    transpose x1, local copies, waits for them, and re-layouts, body(): jnp.einsum('ceaqk,cbsk->ceabqs', left, right, preferred_element_type=jnp....  24.9 us
    reshape x1, local copies, waits for them, and re-layouts, body(): cross.reshape(ch_dev, 2, tiles, tiles, CLASSES * CLASSES)  19.9 us
    reduce_scatter x1, waiting for transfers between devices, body(): return lax.psum_scatter(planes, 'grid', scatter_dimension=0, tiled=True)  19.1 us
    reshape x1, local copies, waits for them, and re-layouts, body(): spectra.reshape(frame_len // 2, 2, step, stn_local, pol_count * chunks)  15.6 us
    all_to_all x1, waiting for transfers between devices, yards_fix(): lax.all_to_all(jnp.stack(jnp.split(array_here, lax.axis_size(axis_tag), 0...  10.8 us
    dot_general x1, matrix products, body(): jnp.einsum('ceaqk,cbsk->ceabqs', left, right, preferred_element_type=jnp....  10.1 us
    dot_general x1, matrix products, body(): planes = jnp.einsum('ckru,ckrew->ucew', rows, spread_cols, precision=high)  9.85 us
  transfers between devices with their start and end apart: 3, of which 2 were waited for; matrix products, arithmetic and copies ran while one was open for 8% of the time, Pallas kernels for 0%

profile of v1, /device:TPU:0, one launch (start us, length us, event | category | flops | bytes accessed | tf_op | source)
XLA Modules:
  0.0 251.7 jit_solution(1560652880823462930)
XLA Ops:
  6.5 2.3 reshape.1068
  8.9 2.4 collective-permute-start
  13.1 4.3 %fusion.100 = f32[3,256,1024]{2,1,0:T(8,128)} fusion(f32[3,9,256]{2,1,0:T(8,128)S(1)} %fusion.53, f32[1024,9,1]{0,1,2:T(8,128)S(1)} %copy-done.9), kind=kOutput, calls=%fused_computation.187 | convolution fusion | flops 84934656 | bytes 3210240 | tf_op jit(solution)/shard_map/qz,czm->cqm/dot_general | solution.py:95
  17.4 0.8 fusion.29
  18.2 1.3 fusion.8
  19.5 0.8 fusion.52
  20.7 1.2 convolution_convert_fusion.1
  21.9 0.5 copy.103
  22.5 15.6 %reshape.1069 = bf16[24,2,8,64,16]{2,1,0,4,3:T(2,128)(2,1)} reshape(bf16[384,128,8]{0,2,1:T(8,128)(2,1)S(1)} %copy.103) | data formatting | bytes 1572864 | tf_op jit(solution)/shard_map/reshape | solution.py:120
  38.1 13.2 %fusion.98 = (bf16[3,2,64,8,16]{3,1,0,4,2:T(2,128)(2,1)S(1)}, bf16[3,2,64,8,16]{3,1,0,4,2:T(2,128)(2,1)S(1)}, bf16[3,2,64,8,16]{3,1,0,4,2:T(2,128)(2,1)}, bf16[3...) fusion(bf16[24,2,64,8,16]{3,1,0,4,2:T(2,128)(2,1)} %bitcast.224), kind=kLoop, calls=%fused_computation.185 | loop fusion | bytes 1572864 | tf_op jit(solution)/shard_map/split | solution.py:19
  51.4 4.0 %copy.104 = bf16[3,2,64,8,16]{2,4,3,1,0:T(8,128)(2,1)S(1)} copy(bf16[3,2,64,8,16]{3,1,0,4,2:T(2,128)(2,1)} %get-tuple-element.12) | data formatting | bytes 196608 | tf_op jit(solution)/shard_map/split | solution.py:19
  55.4 0.7 constant_dynamic-update-slice_fusion.9
  56.1 4.9 %copy.105 = bf16[3,2,64,8,16]{2,4,3,1,0:T(8,128)(2,1)} copy(bf16[3,2,64,8,16]{3,1,0,4,2:T(2,128)(2,1)} %get-tuple-element.11) | data formatting | bytes 196608 | tf_op jit(solution)/shard_map/split | solution.py:19
  61.0 4.9 %copy.106 = bf16[3,2,64,8,16]{2,4,3,1,0:T(8,128)(2,1)} copy(bf16[3,2,64,8,16]{3,1,0,4,2:T(2,128)(2,1)} %get-tuple-element.10) | data formatting | bytes 196608 | tf_op jit(solution)/shard_map/split | solution.py:19
  65.9 4.9 %copy.107 = bf16[3,2,64,8,16]{2,4,3,1,0:T(8,128)(2,1)} copy(bf16[3,2,64,8,16]{3,1,0,4,2:T(2,128)(2,1)} %get-tuple-element.9) | data formatting | bytes 196608 | tf_op jit(solution)/shard_map/split | solution.py:19
  70.8 4.9 %copy.108 = bf16[3,2,64,8,16]{2,4,3,1,0:T(8,128)(2,1)} copy(bf16[3,2,64,8,16]{3,1,0,4,2:T(2,128)(2,1)} %get-tuple-element.8) | data formatting | bytes 196608 | tf_op jit(solution)/shard_map/split | solution.py:19
  75.7 4.9 %copy.109 = bf16[3,2,64,8,16]{2,4,3,1,0:T(8,128)(2,1)} copy(bf16[3,2,64,8,16]{3,1,0,4,2:T(2,128)(2,1)} %get-tuple-element.7) | data formatting | bytes 196608 | tf_op jit(solution)/shard_map/split | solution.py:19
  80.6 2.6 %copy.110 = bf16[3,2,64,8,16]{2,4,3,1,0:T(8,128)(2,1)S(1)} copy(bf16[3,2,64,8,16]{3,1,0,4,2:T(2,128)(2,1)S(1)} %get-tuple-element.6) | data formatting | bytes 196608 | tf_op jit(solution)/shard_map/split | solution.py:19
  83.2 2.6 %copy.111 = bf16[3,2,64,8,16]{2,4,3,1,0:T(8,128)(2,1)S(1)} copy(bf16[3,2,64,8,16]{3,1,0,4,2:T(2,128)(2,1)S(1)} %get-tuple-element.5) | data formatting | bytes 196608 | tf_op jit(solution)/shard_map/split | solution.py:19
  85.9 1.0 constant_dynamic-update-slice_fusion.8
  86.8 1.0 constant_dynamic-update-slice_fusion.7
  87.8 1.0 constant_dynamic-update-slice_fusion.6
  88.7 1.0 constant_dynamic-update-slice_fusion.5
  89.7 1.0 constant_dynamic-update-slice_fusion.4
  90.7 1.4 copy.112
  92.2 6.8 %all-to-all-start = ((bf16[8,3,2,64,128]{4,3,2,1,0:T(8,128)(2,1)}), bf16[8,3,2,64,128]{4,3,2,1,0:T(8,128)(2,1)}, u32[]{:S(2)}, u32[]{:S(2)}) async-start(bf16[8,3,2,64,128]{4,3,2,1,0:T(8,128)(2,1)} %copy.112), calls=%async_computation | async-start | bytes 1572864 | tf_op jit(solution)/shard_map/all_to_all | solution.py:18
  99.6 4.7 %multiply_multiply_fusion = f32[3,256,1024]{2,1,0:T(8,128)S(1)} fusion(f32[3,256,1024]{2,1,0:T(8,128)} %fusion.100, f32[3,9,256]{2,1,0:T(8,128)S(1)} %copy-done.6, f32[1024,9,1]{0,1,2:T(8,128)S(1)} %copy-done.8), kind=kOutput, calls=%fused_computation.12 | convolution fusion | flops 86507520 | bytes 6355968 | tf_op jit(solution)/shard_map/qz,czm->cqm/dot_general | solution.py:98
  104.3 5.4 %iota_compare_fusion = pred[3,2,256,16,128]{4,3,2,0,1:T(8,128)(4,1)} fusion(s32[3,2,256,16]{3,2,0,1:T(8,128)S(1)} %iota_add_fusion), kind=kLoop, calls=%fused_computation.4 | loop fusion | flops 3145728 | bytes 3244032 | tf_op jit(solution)/shard_map/eq | solution.py:177
  109.7 10.8 %all-to-all-done = bf16[8,3,2,64,128]{4,3,2,1,0:T(8,128)(2,1)} async-done(((bf16[8,3,2,64,128]{4,3,2,1,0:T(8,128)(2,1)}), bf16[8,3,2,64,128]{4,3,2,1,0:T(8,128)(2,1)}, u32[]{:S(2)}, u32[]{:S(2)}) %all-to-all-start) | async-done | bytes 786464 | tf_op jit(solution)/shard_map/all_to_all | solution.py:18
  120.5 1.2 copy.113
  121.7 0.4 fusion.26
  122.2 1.0 slice_bitcast_fusion.7
  123.6 10.1 %convolution_bitcast_fusion = f32[3,2,16,16,32,32]{4,5,2,1,3,0:T(8,128)} fusion(bf16[3,16,32,256,1,1]{3,2,0,1,5,4:T(8,128)(2,1)S(1)} %get-tuple-element.15, bf16[3,1,16,32,256]{4,3,0,2,1:T(8,128)(2,1)S(1)} %get-tuple-element.21, bf16[3,1,16,32,256]{4,3,0,2,1:T(8,128)(2,1)S(1)} %get-tuple-element.16), kind=kOutput, calls=%fused_computation.5 | convolution fusion | flops 806092800 | bytes 8650752 | tf_op jit(solution)/shard_map/ceaqk,cbsk->ceabqs/dot_general | solution.py:146
  133.7 24.9 %copy.125 = f32[3,2,16,16,32,32]{5,4,3,2,1,0:T(8,128)} copy(f32[3,2,16,16,32,32]{4,5,2,1,3,0:T(8,128)} %convolution_bitcast_fusion) | data formatting | bytes 12582912 | tf_op jit(solution)/shard_map/ceaqk,cbsk->ceabqs/transpose | solution.py:146
  158.5 19.9 %reshape.1072 = f32[3,2,16,16,1024]{4,3,2,1,0:T(8,128)} reshape(f32[3,2,16,16,32,32]{5,4,3,2,1,0:T(8,128)} %copy.125) | data formatting | bytes 12582912 | tf_op jit(solution)/shard_map/reshape | solution.py:151
  178.4 1.6 fusion.36
  180.1 1.3 bitcast_select_fusion
  181.4 0.6 fusion.16
  182.0 1.7 fusion.18
  183.7 3.0 %copy.120 = f32[3,2,16,32,32]{4,3,2,1,0:T(8,128)} copy(f32[3,2,16,32,32]{3,4,1,0,2:T(8,128)} %fusion.18) | data formatting | bytes 786432 | tf_op jit(solution)/shard_map/ceaqj,ajs->ceaqs/transpose | solution.py:160
  186.7 2.1 reshape.1071
  188.8 1.5 fusion.6
  190.4 6.8 %fusion.23 = f32[3,2,16,16,256]{4,3,2,1,0:T(8,128)} fusion(f32[3,2,16,16,1024]{4,3,2,1,0:T(8,128)} %reshape.1072, f32[3,256,1024]{2,1,0:T(8,128)S(1)} %multiply_multiply_fusion, f32[3,2,16,256]{3,2,1,0:T(8,128)S(1)} %fusion.6, pred[16,16]{1,0:T(8,128)(4,1)S(1)} %copy-done.14), kind=kOutput, calls=%fused_computation.34 | convolution fusion | flops 2416312320 | bytes 11108608 | tf_op jit(solution)/shard_map/ceabm,cmn->ceabn/dot_general | solution.py:149
  197.2 8.4 %reshape.1073 = f32[3,2,256,16,16]{4,3,2,1,0:T(8,128)} reshape(f32[3,2,16,16,256]{4,3,2,1,0:T(8,128)} %fusion.23) | data formatting | bytes 3145728 | tf_op jit(solution)/shard_map/reshape | solution.py:174
  205.6 9.3 %fusion.2 = f32[3,256,128,2,16]{2,4,3,1,0:T(8,128)} fusion(f32[3,2,256,16,16]{4,3,2,1,0:T(8,128)} %reshape.1073, pred[3,2,256,16,128]{4,3,2,0,1:T(8,128)(4,1)S(1)} %copy-done.2), kind=kOutput, calls=%fused_computation.2 | convolution fusion | flops 301989888 | bytes 15728640 | tf_op jit(solution)/shard_map/cekrt,cktw->ckrew/dot_general | solution.py:179
  214.9 9.8 %fusion = f32[3,2,128,128,1]{3,2,1,4,0:T(8,128)S(1)} fusion(f32[3,256,128,2,16]{2,4,3,1,0:T(8,128)} %fusion.2, pred[3,2,256,16,128]{4,3,2,0,1:T(8,128)(4,1)S(1)} %copy-done.2), kind=kOutput, calls=%fused_computation | convolution fusion | flops 2415919104 | bytes 14548992 | tf_op jit(solution)/shard_map/ckru,ckrew->ucew/dot_general | solution.py:180
  224.8 0.9 copy.128
  225.7 19.1 %reduce-scatter.2.cloned.1.call-done = f32[32,3,256]{2,0,1:T(8,128)} async-done(((f32[128,3,256]{2,0,1:T(8,128)}), f32[32,3,256]{2,0,1:T(8,128)}) %reduce-scatter.2.cloned.1.call-update) | async-done | bytes 98320 | tf_op jit(solution)/shard_map/reduce_scatter | solution.py:182
  (98 shorter events, 3.1 us)
Async XLA Ops:
  6.5 5.2 %copy-start = (f32[8,7]{1,0:T(8,128)S(1)}, f32[8,7]{1,0:T(8,128)}, u32[]{:S(2)}) copy-start(f32[8,7]{1,0:T(8,128)} %param.18) | copy-start | bytes 676
  6.5 6.3 %copy-start.12 = (f32[16,256,1]{1,0,2:T(8,128)S(1)}, f32[16,256,1]{1,0,2:T(8,128)}, u32[]{:S(2)}) copy-start(f32[16,256,1]{1,0,2:T(8,128)} %constant.175) | copy-start | bytes 49156
  6.5 6.5 %copy-start.9 = (f32[1024,9,1]{0,1,2:T(8,128)S(1)}, f32[1024,9,1]{0,1,2:T(8,128)}, u32[]{:S(2)}) copy-start(f32[1024,9,1]{0,1,2:T(8,128)} %constant.176) | copy-start | bytes 110596
  6.5 4.8 %copy-start.13 = (f32[16,48]{1,0:T(8,128)S(1)}, f32[16,48]{1,0:T(8,128)}, u32[]{:S(2)}) copy-start(f32[16,48]{1,0:T(8,128)} %param.15) | copy-start | bytes 9220
  6.5 5.9 %copy-start.15 = (s32[3,2,136]{2,1,0:T(2,128)S(1)}, s32[3,2,136]{2,1,0:T(2,128)}, u32[]{:S(2)}) copy-start(s32[3,2,136]{2,1,0:T(2,128)} %param.17) | copy-start | bytes 9796
  8.9 11.4 %collective-permute-start = (bf16[128,768]{1,0:T(8,128)(2,1)S(1)}, bf16[128,768]{1,0:T(8,128)(2,1)S(1)}, u32[]{:S(2)}, u32[]{:S(2)}) collective-permute-start(bf16[128,768]{1,0:T(8,128)(2,1)S(1)} %slice.169), channel_id=1, source_target_pairs={{0,1},{1,2},{2,3},{4,5},{5,6},{6,7},{8,9},{9,10},{10,11},{12,13},{... | collective-permute-start | bytes 589832 | tf_op jit(solution)/shard_map/ppermute | solution.py:34
  12.2 5.2 %copy-start.7 = (f32[136,256,1]{1,0,2:T(8,128)S(1)}, f32[136,256,1]{1,0,2:T(8,128)}, u32[]{:S(2)}) copy-start(f32[136,256,1]{1,0,2:T(8,128)} %constant.174) | copy-start | bytes 417796
  12.2 5.2 %copy-start.25 = (s32[256]{0:T(256)S(1)}, s32[256]{0:T(256)}, u32[]{:S(2)}) copy-start(s32[256]{0:T(256)} %constant.139.clone) | copy-start | bytes 3076
  12.7 5.5 %copy-start.17 = (f32[384]{0:T(512)S(1)}, f32[384]{0:T(512)}, u32[]{:S(2)}) copy-start(f32[384]{0:T(512)} %constant.173) | copy-start | bytes 4612
  12.7 5.5 %copy-start.18 = (f32[384]{0:T(512)S(1)}, f32[384]{0:T(512)}, u32[]{:S(2)}) copy-start(f32[384]{0:T(512)} %constant.171) | copy-start | bytes 4612
  12.7 5.5 %copy-start.19 = (f32[384]{0:T(512)S(1)}, f32[384]{0:T(512)}, u32[]{:S(2)}) copy-start(f32[384]{0:T(512)} %constant.169) | copy-start | bytes 4612
  12.7 5.5 %copy-start.20 = (f32[384]{0:T(512)S(1)}, f32[384]{0:T(512)}, u32[]{:S(2)}) copy-start(f32[384]{0:T(512)} %constant.167) | copy-start | bytes 4612
  12.7 5.5 %copy-start.21 = (f32[384]{0:T(512)S(1)}, f32[384]{0:T(512)}, u32[]{:S(2)}) copy-start(f32[384]{0:T(512)} %constant.165) | copy-start | bytes 4612
  12.7 5.5 %copy-start.22 = (f32[384]{0:T(512)S(1)}, f32[384]{0:T(512)}, u32[]{:S(2)}) copy-start(f32[384]{0:T(512)} %constant.163) | copy-start | bytes 4612
  12.7 5.5 %copy-start.23 = (f32[384]{0:T(512)S(1)}, f32[384]{0:T(512)}, u32[]{:S(2)}) copy-start(f32[384]{0:T(512)} %constant.161) | copy-start | bytes 4612
  12.8 5.4 %copy-start.24 = (f32[384]{0:T(512)S(1)}, f32[384]{0:T(512)}, u32[]{:S(2)}) copy-start(f32[384]{0:T(512)} %constant.159) | copy-start | bytes 4612
  13.1 6.5 %copy-start.11 = (f32[16,256,1]{1,0,2:T(8,128)S(1)}, f32[16,256,1]{1,0,2:T(8,128)}, u32[]{:S(2)}) copy-start(f32[16,256,1]{1,0,2:T(8,128)} %constant.177) | copy-start | bytes 49156
  83.2 2.6 %copy-start.3 = (bf16[8,3,2,64,128]{3,4,2,1,0:T(8,128)(2,1)S(1)}, bf16[8,3,2,64,128]{3,4,2,1,0:T(8,128)(2,1)}, u32[]{:S(2)}) copy-start(bf16[8,3,2,64,128]{3,4,2,1,0:T(8,128)(2,1)} %constant_dynamic-update-slice_fusion.9) | copy-start | bytes 2359300
  90.7 8.5 %copy-start.16 = (s32[2,512]{1,0:T(2,128)S(1)}, s32[2,512]{1,0:T(2,128)}, u32[]{:S(2)}) copy-start(s32[2,512]{1,0:T(2,128)} %param.16) | copy-start | bytes 12292
  90.7 8.6 %copy-start.10 = (s32[3,2,256]{2,0,1:T(4,128)S(1)}, s32[3,2,256]{2,0,1:T(4,128)}, u32[]{:S(2)}) copy-start(s32[3,2,256]{2,0,1:T(4,128)} %fusion.29) | copy-start | bytes 18436
  92.2 7.4 %copy-start.6 = (f32[3,9,256]{2,1,0:T(8,128)S(1)}, f32[3,9,256]{2,1,0:T(8,128)}, u32[]{:S(2)}) copy-start(f32[3,9,256]{2,1,0:T(8,128)} %fusion.52) | copy-start | bytes 82948
  92.2 7.4 %copy-start.8 = (f32[1024,9,1]{0,1,2:T(8,128)S(1)}, f32[1024,9,1]{0,1,2:T(8,128)}, u32[]{:S(2)}) copy-start(f32[1024,9,1]{0,1,2:T(8,128)} %constant.178) | copy-start | bytes 110596
  92.2 28.4 %all-to-all-start = ((bf16[8,3,2,64,128]{4,3,2,1,0:T(8,128)(2,1)}), bf16[8,3,2,64,128]{4,3,2,1,0:T(8,128)(2,1)}, u32[]{:S(2)}, u32[]{:S(2)}) async-start(bf16[8,3,2,64,128]{4,3,2,1,0:T(8,128)(2,1)} %copy.112), calls=%async_computation | async-start | bytes 1572864 | tf_op jit(solution)/shard_map/all_to_all | solution.py:18
  99.0 145.9 %reduce-scatter.2.cloned.1.call-start = ((), (), s32[]{:S(2)}) async-start(), calls=%async_computation.2 | async-start | bytes 491520 | tf_op jit(solution)/shard_map/reduce_scatter | solution.py:182
  178.4 1.6 copy-start.4
  178.4 1.6 copy-start.5
  178.4 1.6 copy-start.26
  188.8 1.6 copy-start.14
  197.2 8.4 %copy-start.2 = (pred[3,2,256,16,128]{4,3,2,0,1:T(8,128)(4,1)S(1)}, pred[3,2,256,16,128]{4,3,2,0,1:T(8,128)(4,1)}, u32[]{:S(2)}) copy-start(pred[3,2,256,16,128]{4,3,2,0,1:T(8,128)(4,1)} %iota_compare_fusion) | copy-start | bytes 9437188
  214.9 29.9 %copy-start.1 = (f32[8,7]{1,0:T(8,128)S(1)}, f32[8,7]{1,0:T(8,128)}, u32[]{:S(2)}) copy-start(f32[8,7]{1,0:T(8,128)} %param.18) | copy-start | bytes 676
Sparse Core Ops, SparseCore 0:
  225.9 18.9 reduce-scatter.1
